TPU v7x, 32 devices: a whole 2x2x4 slice. The times are simulated.
32 devices in a mesh: grp: 4 (over y, core), wide: 8 (over z, x).
Axes of the slice: x: 2, y: 2, z: 4, core: 2. Of those that a mesh axis runs over, the one named last changes fastest.
Arguments:
- coefficients: bfloat16 [512, 2, 128, 512], P(('grp', 'wide')), may hold values from -6 to 6
- source_blocks: bfloat16 [2, 512, 2, 128, 256], P(None, ('grp', 'wide')), may hold values from -0.25 to 0.25
- target_blocks: bfloat16 [3, 512, 2, 128, 256], P(None, ('grp', 'wide')), may hold values from -0.25 to 0.25
- pair_tables: int32 [2, 32, 16], P(None, ('grp', 'wide')), may hold values from 0 to 15, each once within a row
Outputs:
- target_coeffs: bfloat16 [512, 2, 128, 512], P(('grp', 'wide'))
Inputs may be any that keep to these rules, and one draw needn't show every extreme that they name: Each row pair_tables[s, d] is a permutation of the numbers 0 to 15.
All inputs are finite; a program needn't handle non-finite values.
Results may differ from a plain program's by a relative error of at most 0.007.
Values may be sent and summed in bfloat16 or wider, within the bound.
A program may use at most 128 MiB of HBM per device.

v0:
```python
import jax
import jax.numpy as jnp
from jax import lax
from jax.sharding import PartitionSpec as P


def swapped(value, axis, distance):
    mask = 2**distance
    pairs = [(source, source ^ mask) for source in range(lax.axis_size(axis))]
    return lax.ppermute(value, axis, pairs)


def complex_terms(blocks, stacked):
    real_part = jnp.einsum(
        "nij,njk->nik", blocks[:, 0], stacked[:, 0], preferred_element_type=jnp.float32
    ) - jnp.einsum("nij,njk->nik", blocks[:, 1], stacked[:, 1], preferred_element_type=jnp.float32)
    imag_part = jnp.einsum(
        "nij,njk->nik", blocks[:, 0], stacked[:, 1], preferred_element_type=jnp.float32
    ) + jnp.einsum("nij,njk->nik", blocks[:, 1], stacked[:, 0], preferred_element_type=jnp.float32)
    return jnp.stack([real_part, imag_part], axis=1)


def source_level(local_boxes, local_blocks, order_row):
    picked = jnp.take(local_boxes, order_row, axis=0)
    count = picked.shape[0]
    paired = picked.reshape((count // 2, 2) + picked.shape[1:])
    joined = jnp.concatenate([paired[:, 0], paired[:, 1]], axis=2)
    joined = jnp.repeat(joined, 2, axis=0)
    return complex_terms(local_blocks, joined).astype(jnp.bfloat16)


def target_levels(state, target_blocks):
    bit_count = lax.axis_size("grp").bit_length() - 1
    group_id = lax.axis_index("grp")
    for layer_idx in range(target_blocks.shape[0]):
        bit_num = layer_idx % bit_count
        partner = swapped(state, "grp", bit_num)
        is_upper = group_id >> bit_num & 1 == 1
        level_blocks = target_blocks[layer_idx]
        lower_part = jnp.where(is_upper, partner, state)
        upper_part = jnp.where(is_upper, state, partner)
        joined = jnp.concatenate([lower_part, upper_part], axis=2)
        state = complex_terms(level_blocks, joined).astype(jnp.bfloat16)
    return state


def on_device(coefficients, source_blocks, target_blocks, pair_tables):
    current = coefficients
    for layer_idx in range(source_blocks.shape[0]):
        current = source_level(current, source_blocks[layer_idx], pair_tables[layer_idx, 0])
    current = lax.all_to_all(current, "wide", split_axis=0, concat_axis=0, tiled=True)
    return target_levels(current, target_blocks)


def solution(mesh):
    in_specs = (
        P(("grp", "wide"), None, None, None),
        P(None, ("grp", "wide"), None, None, None),
        P(None, ("grp", "wide"), None, None, None),
        P(None, ("grp", "wide"), None),
    )
    out_specs = P(("grp", "wide"), None, None, None)
    return jax.shard_map(
        on_device, mesh=mesh, in_specs=in_specs, out_specs=out_specs, check_vma=False
    )
```

profile of v0, /device:TPU:9, one launch (start us, length us, event | category | flops | bytes accessed | tf_op | source)
XLA Modules:
  0.0 311.4 jit_solution(9663648712112545328)
XLA Ops:
  0.0 0.7 compare_and_fusion
  0.7 5.0 %gather_fusion = bf16[16,2,128,512]{3,2,1,0:T(8,128)(2,1)} fusion(bf16[16,2,128,512]{3,2,1,0:T(8,128)(2,1)} %param.6, s32[1024]{0:T(1024)S(1)} %get-tuple-element.28), kind=kCustom, calls=%fused_computation.clone | custom fusion | bytes 8388672 | tf_op jit(solution)/shard_map/jit(_take)/gather | solution.py:24
  5.7 2.6 broadcast_select_fusion.1
  8.4 0.5 slice_bitcast_fusion.15
  8.8 2.4 pad_maximum_fusion.3
  11.2 6.3 %copy.24 = bf16[8,2,256,512]{2,3,0,1:T(8,128)(2,1)} copy(bf16[8,2,256,512]{3,2,1,0:T(8,128)(2,1)} %pad_maximum_fusion.3) | data formatting | bytes 8388608 | tf_op jit(solution)/shard_map/concatenate | solution.py:27
  17.5 2.7 fusion.55
  20.2 0.4 copy_bitcast_fusion.1
  20.6 6.4 %broadcast_in_dim.15 = bf16[8,2,2,256,512]{3,4,1,0,2:T(8,128)(2,1)} broadcast(bf16[8,2,256,512]{2,3,0,1:T(8,128)(2,1)} %copy.24), dimensions={0,2,3,4} | broadcast | bytes 12582912 | tf_op jit(solution)/shard_map/broadcast_in_dim | solution.py:28
  27.0 3.6 %fusion.9 = f32[16,512,128]{2,1,0:T(8,128)S(1)} fusion(bf16[16,2,256,512]{2,3,0,1:T(8,128)(2,1)} %bitcast.169, bf16[16,2,128,256]{3,2,0,1:T(8,128)(2,1)S(1)} %get-tuple-element.30), kind=kOutput, calls=%fused_computation.49 | convolution fusion | flops 536870912 | bytes 9437184 | tf_op jit(solution)/shard_map/nij,njk->nik/dot_general | solution.py:19
  30.6 1.0 copy-done
  31.6 1.3 fusion.10
  32.9 1.3 fusion.18
  34.1 1.3 fusion.17
  35.4 2.4 pad_maximum_fusion.4
  37.8 5.2 %gather_fusion.1 = bf16[16,2,128,512]{2,3,1,0:T(8,128)(2,1)} fusion(bf16[16,2,128,512]{2,3,0,1:T(8,128)(2,1)} %pad_maximum_fusion.4, s32[1024]{0:T(1024)S(1)} %get-tuple-element.27), kind=kCustom, calls=%fused_computation.1.clone | custom fusion | bytes 8388672 | tf_op jit(solution)/shard_map/jit(_take)/gather | solution.py:24
  43.0 2.6 broadcast_select_fusion
  45.7 0.4 slice_bitcast_fusion.13
  46.1 0.6 pad_maximum_fusion.5
  46.7 2.3 copy.27
  49.1 6.4 %broadcast_in_dim.16 = bf16[8,2,2,256,512]{3,4,1,0,2:T(8,128)(2,1)} broadcast(bf16[8,2,256,512]{2,3,0,1:T(8,128)(2,1)} %copy.27), dimensions={0,2,3,4} | broadcast | bytes 12582912 | tf_op jit(solution)/shard_map/broadcast_in_dim | solution.py:28
  55.4 3.6 %fusion.13 = f32[16,512,128]{2,1,0:T(8,128)S(1)} fusion(bf16[16,2,256,512]{2,3,0,1:T(8,128)(2,1)} %bitcast.173, bf16[16,2,128,256]{3,2,0,1:T(8,128)(2,1)S(1)} %get-tuple-element.29), kind=kOutput, calls=%fused_computation.53 | convolution fusion | flops 536870912 | bytes 9437184 | tf_op jit(solution)/shard_map/nij,njk->nik/dot_general | solution.py:19
  59.0 1.1 copy-done.1
  60.1 1.3 fusion.14
  61.3 1.5 fusion.20
  62.8 1.3 fusion.19
  64.1 0.4 pad_maximum_fusion.6
  64.5 0.4 copy.29
  64.9 96.9 %all_to_all.5 = bf16[16,2,128,512]{2,3,1,0:T(8,128)(2,1)} all-to-all(bf16[16,2,128,512]{2,3,1,0:T(8,128)(2,1)S(1)} %copy.29), channel_id=1, replica_groups=mesh['grp'=4,'wide'=8] {'wide'}, dimensions={0} | all-to-all | bytes 8388608 | tf_op jit(solution)/shard_map/all_to_all | solution.py:51
  161.8 6.2 %copy.30 = bf16[16,2,128,512]{3,2,0,1:T(8,128)(2,1)} copy(bf16[16,2,128,512]{2,3,1,0:T(8,128)(2,1)} %all_to_all.5) | data formatting | bytes 8388608 | tf_op jit(solution)/shard_map/all_to_all | solution.py:51
  168.0 2.2 collective-permute-start
  170.2 5.7 %fusion.54 = (bf16[1,16,2,128,256]{4,3,2,1,0:T(8,128)(2,1)S(1)}, bf16[1,16,2,128,256]{4,3,2,1,0:T(8,128)(2,1)}, bf16[1,16,2,128,256]{4,3,2,1,0:T(8,128)(2,1)}) fusion(bf16[3,16,2,128,256]{4,3,2,1,0:T(8,128)(2,1)} %param.8), kind=kLoop, calls=%fused_computation.107 | loop fusion | bytes 12582912 | tf_op jit(solution)/shard_map/slice | solution.py:39
  175.9 0.1 copy.58
  176.0 1.3 collective-permute-done
  177.3 0.7 copy-done.4
  178.1 2.5 broadcast_select_fusion.6
  180.6 0.9 fusion.29
  181.5 1.3 fusion.30
  182.8 1.0 fusion.21
  183.7 1.0 fusion.24
  184.7 0.0 copy-start.2
  184.7 2.6 pad_maximum_fusion.7
  187.3 0.0 copy-done.2
  187.3 1.3 collective-permute-start.1
  188.6 1.9 copy.59
  190.4 89.4 %collective-permute-done.1 = bf16[16,2,128,512]{3,2,0,1:T(8,128)(2,1)} collective-permute-done((bf16[16,2,128,512]{3,2,0,1:T(8,128)(2,1)}, bf16[16,2,128,512]{3,2,0,1:T(8,128)(2,1)}, u32[]{:S(2)}, u32[]{:S(2)}) %collective-permute-start.1) | collective-permute-done | bytes 4194336 | tf_op jit(solution)/shard_map/ppermute | solution.py:10
  279.8 2.5 broadcast_select_fusion.2
  282.3 0.9 fusion.31
  283.3 1.3 fusion.32
  284.5 1.0 fusion.22
  285.6 1.0 fusion.25
  286.6 0.0 copy-start.5
  286.6 0.4 pad_maximum_fusion.8
  287.0 0.8 collective-permute-start.2
  287.8 0.3 copy-done.5
  288.2 0.1 copy.57
  288.3 6.3 %collective-permute-done.2 = bf16[16,2,128,512]{3,2,0,1:T(8,128)(2,1)S(1)} collective-permute-done((bf16[16,2,128,512]{3,2,0,1:T(8,128)(2,1)S(1)}, bf16[16,2,128,512]{3,2,0,1:T(8,128)(2,1)S(1)}, u32[]{:S(2)}, u32[]{:S(2)}) %collective-permute-start.2) | collective-permute-done | bytes 4194336 | tf_op jit(solution)/shard_map/ppermute | solution.py:10
  294.6 0.6 broadcast_select_fusion.4
  295.2 2.1 fusion.34
  297.3 1.7 fusion.35
  299.1 1.8 fusion.26
  300.9 1.8 fusion.23
  302.6 2.3 pad_maximum_fusion.9
  305.0 6.4 %copy.40 = bf16[16,2,128,512]{3,2,1,0:T(8,128)(2,1)} copy(bf16[16,2,128,512]{2,3,0,1:T(8,128)(2,1)} %pad_maximum_fusion.9) | data formatting | bytes 8388608 | tf_op jit(solution)/shard_map/stack | solution.py:20
  (6 shorter events, 0.0 us)
Async XLA Ops:
  27.0 4.6 %copy-start = (bf16[8,2,2,256,512]{3,4,1,0,2:T(8,128)(2,1)S(1)}, bf16[8,2,2,256,512]{3,4,1,0,2:T(8,128)(2,1)}, u32[]{:S(2)}) copy-start(bf16[8,2,2,256,512]{3,4,1,0,2:T(8,128)(2,1)} %broadcast_in_dim.15) | copy-start | bytes 25165828
  55.4 4.6 %copy-start.1 = (bf16[8,2,2,256,512]{3,4,1,0,2:T(8,128)(2,1)S(1)}, bf16[8,2,2,256,512]{3,4,1,0,2:T(8,128)(2,1)}, u32[]{:S(2)}) copy-start(bf16[8,2,2,256,512]{3,4,1,0,2:T(8,128)(2,1)} %broadcast_in_dim.16) | copy-start | bytes 25165828
  168.0 9.3 %collective-permute-start = (bf16[16,2,128,512]{3,2,0,1:T(8,128)(2,1)}, bf16[16,2,128,512]{3,2,0,1:T(8,128)(2,1)}, u32[]{:S(2)}, u32[]{:S(2)}) collective-permute-start(bf16[16,2,128,512]{3,2,0,1:T(8,128)(2,1)} %copy.30), channel_id=1, source_target_pairs={{0,8},{8,0},{16,24},{24,16},{1,9},{9,1},{17,25},{25,17},{2,10},{10... | collective-permute-start | bytes 12582920 | tf_op jit(solution)/shard_map/ppermute | solution.py:10
  175.9 2.2 copy-start.4
  184.7 2.6 copy-start.2
  187.3 92.5 %collective-permute-start.1 = (bf16[16,2,128,512]{3,2,0,1:T(8,128)(2,1)}, bf16[16,2,128,512]{3,2,0,1:T(8,128)(2,1)}, u32[]{:S(2)}, u32[]{:S(2)}) collective-permute-start(bf16[16,2,128,512]{3,2,0,1:T(8,128)(2,1)} %pad_maximum_fusion.7), channel_id=1, source_target_pairs={{0,16},{8,24},{16,0},{24,8},{1,17},{9,25},{17,1},{25,9},{2,18},{10... | collective-permute-start | bytes 12582920 | tf_op jit(solution)/shard_map/ppermute | solution.py:10
  188.6 91.2 %copy-start.3 = (bf16[16,1,128,512]{3,2,0,1:T(8,128)(2,1)S(1)}, bf16[16,1,128,512]{3,2,0,1:T(8,128)(2,1)}, u32[]{:S(2)}) copy-start(bf16[16,1,128,512]{3,2,0,1:T(8,128)(2,1)} %copy-done.2) | copy-start | bytes 6291460
  286.6 1.6 copy-start.5
  287.0 7.6 %collective-permute-start.2 = (bf16[16,2,128,512]{3,2,0,1:T(8,128)(2,1)S(1)}, bf16[16,2,128,512]{3,2,0,1:T(8,128)(2,1)S(1)}, u32[]{:S(2)}, u32[]{:S(2)}) collective-permute-start(bf16[16,2,128,512]{3,2,0,1:T(8,128)(2,1)S(1)} %pad_maximum_fusion.8), channel_id=1, source_target_pairs={{0,8},{8,0},{16,24},{24,16},{1,9},{9,1},{17,25},{25,17},{2,10},{10... | collective-permute-start | bytes 12582920 | tf_op jit(solution)/shard_map/ppermute | solution.py:10
where the time goes:
time: 314 us; the launch traced here: 311 us
  waiting for transfers between devices  97 us (31%)
  blocking collectives  96.9 us (31%)
  local copies, waits for them, and re-layouts  59.6 us (19%)
  matrix products  30.7 us (10%)
  other arithmetic  22.6 us (7%)
  starting transfers between devices  4.28 us (1%)
    ppermute x3, waiting for transfers between devices, swapped(): return lax.ppermute(value, axis, pairs)  97 us
    all_to_all x1, blocking collectives, on_device(): lax.all_to_all(current, 'wide', split_axis=0, concat_axis=0, tiled=True)  96.9 us
    broadcast_in_dim x2, local copies, waits for them, and re-layouts, source_level(): joined = jnp.repeat(joined, 2, axis=0)  12.7 us
    dot_general x5, matrix products, complex_terms(): jnp.einsum('nij,njk->nik', blocks[:, 1], stacked[:, 0], preferred_element...  11.9 us
    gather x2, local copies, waits for them, and re-layouts, source_level(): picked = jnp.take(local_boxes, order_row, axis=0)  10.2 us
    concatenate x2, local copies, waits for them, and re-layouts, source_level(): joined = jnp.concatenate([paired[:, 0], paired[:, 1]], axis=2)  8.62 us
    another operation x5, other arithmetic, complex_terms(): return jnp.stack([real_part, imag_part], axis=1)  8.06 us
    another operation x2, local copies, waits for them, and re-layouts, complex_terms(): return jnp.stack([real_part, imag_part], axis=1)  6.84 us
  transfers between devices with their start and end apart: 3, of which 3 were waited for; matrix products, arithmetic and copies ran while one was open for 3% of the time, Pallas kernels for 0%

commit v1 on v0

v1 whole, which is shorter than its diff:
```python
import functools

import jax
import jax.numpy as jnp
from jax import lax
from jax.experimental import pallas as pl
from jax.experimental.pallas import tpu as pltpu
from jax.sharding import PartitionSpec as P

MESH = pl.DeviceIdType.MESH
LOOK_CHUNKS = 2


def flipped(index, other, size):
    total, bit = 0, 1
    while bit < size:
        total = total + ((index // bit) % 2 + (other // bit) % 2) % 2 * bit
        bit *= 2
    return total


def product(matrix, upper_r, lower_r, upper_i, lower_i):
    cols = upper_r.shape[-1]
    right = jnp.concatenate(
        [jnp.concatenate([upper_r, lower_r], axis=0), jnp.concatenate([upper_i, lower_i], axis=0)],
        axis=1,
    )
    both = jnp.dot(matrix, right, preferred_element_type=jnp.float32)
    rank = upper_r.shape[0]
    pairs = []
    for base in range(0, both.shape[0], 2 * rank):
        top, low = both[base : base + rank], both[base + rank : base + 2 * rank]
        real = top[:, :cols] - low[:, cols:]
        imag = top[:, cols:] + low[:, :cols]
        pairs.append((real.astype(jnp.bfloat16), imag.astype(jnp.bfloat16)))
    return pairs


def kernel(
    n_grp, n_wide, tables, coef, sb, tb, out,
    x1, x2, v, a_send, a_recv, l_send, l_recv,
):
    boxes, _, rank, width = coef.shape
    src_levels, tgt_levels = sb.shape[0], tb.shape[0]
    chunks, cols = x1.shape[0], x1.shape[-1]
    per = boxes // n_wide
    units = chunks * n_wide
    bits = n_grp.bit_length() - 1
    g = lax.axis_index("grp")
    w = lax.axis_index("wide")
    mask = [2 ** (t % bits) for t in range(tgt_levels)]
    side = [(g // b) % 2 for b in mask]
    partner = [g + b * (1 - 2 * s) for b, s in zip(mask, side)]

    barrier = pltpu.get_barrier_semaphore()
    for d in range(1, n_wide):
        pl.semaphore_signal(
            barrier, inc=1, device_id=(g, flipped(w, d, n_wide)), device_id_type=MESH
        )
    for t in range(min(tgt_levels, bits)):
        pl.semaphore_signal(barrier, inc=1, device_id=(partner[t], w), device_id_type=MESH)
    pl.semaphore_wait(barrier, n_wide - 1 + min(tgt_levels, bits))

    def source(c):
        for s in range(src_levels):
            def step(m, carry, s=s):
                qa, qb = tables[s, 0, 2 * m], tables[s, 0, 2 * m + 1]
                if s == 0:
                    at = pl.ds(pl.multiple_of(c * cols, cols), cols)
                    parts = [coef[q, h, :, at] for h in range(2) for q in (qa, qb)]
                else:
                    prev = x1 if s % 2 == 1 else x2
                    parts = [prev[c, q, h] for h in range(2) for q in (qa, qb)]
                dest = x1 if s % 2 == 0 else x2
                matrix = sb[s, pl.ds(2 * m, 2)].reshape(4 * rank, 2 * rank)
                for i, (real, imag) in enumerate(product(matrix, *parts)):
                    dest[c, 2 * m + i, 0] = real
                    dest[c, 2 * m + i, 1] = imag
                return carry

            lax.fori_loop(0, boxes // 2, step, 0)
        last = x1 if src_levels % 2 == 1 else x2
        v[0, c * n_wide, side[0]] = last[c, pl.ds(w * per, per)]

    def across(u):
        c, d = u // n_wide, u % n_wide
        peer = flipped(w, d, n_wide)
        last = x1 if src_levels % 2 == 1 else x2
        return pltpu.make_async_remote_copy(
            src_ref=last.at[c, pl.ds(peer * per, per)],
            dst_ref=v.at[0, u, side[0]],
            send_sem=a_send.at[u],
            recv_sem=a_recv.at[u],
            device_id=(g, peer),
            device_id_type=MESH,
        )

    def exchange(t, u):
        return pltpu.make_async_remote_copy(
            src_ref=v.at[t, u, side[t]],
            dst_ref=v.at[t, u, side[t]],
            send_sem=l_send.at[t, u],
            recv_sem=l_recv.at[t, u],
            device_id=(partner[t], w),
            device_id_type=MESH,
        )

    def send_chunk(c):
        def step(d, carry):
            across(c * n_wide + d).start()
            return carry

        lax.fori_loop(1, n_wide, step, 0)

    look = min(LOOK_CHUNKS, chunks)

    def lead(c, carry):
        source(c)

        @pl.when(c < look)
        def _():
            send_chunk(c)

        return carry

    lax.fori_loop(0, chunks, lead, 0)

    def arrive(u):
        @pl.when(u % n_wide > 0)
        def _():
            across(u).wait_recv()

        later = u + look * n_wide

        @pl.when((u % n_wide > 0) & (later < units))
        def _():
            across(later).start()

        exchange(0, u).start()

    def target(t, u):
        exchange(t, u).wait_recv()
        c, d = u // n_wide, u % n_wide
        base = flipped(w, d, n_wide) * per
        for m in range(per):
            matrix = tb[t, base + m].reshape(2 * rank, 2 * rank)
            parts = [v[t, u, half, m, h] for h in range(2) for half in range(2)]
            [(real, imag)] = product(matrix, *parts)
            if t + 1 < tgt_levels:
                v[t + 1, u, side[t + 1], m, 0] = real
                v[t + 1, u, side[t + 1], m, 1] = imag
            else:
                at = pl.ds(pl.multiple_of(c * cols, cols), cols)
                out[base + m, 0, :, at] = real
                out[base + m, 1, :, at] = imag
        if t + 1 < tgt_levels:
            exchange(t + 1, u).start()

    lags, lag = [], 0
    for t in range(tgt_levels):
        lag += 1 if mask[t] == 1 else 2
        lags.append(lag)

    def main(s, carry):
        @pl.when(s < units)
        def _():
            arrive(s)

        for t in range(tgt_levels):
            @pl.when((s >= lags[t]) & (s < units + lags[t]))
            def _(t=t):
                target(t, s - lags[t])

        return carry

    lax.fori_loop(0, units + lags[-1], main, 0)

    def drain(u, carry):
        @pl.when(u % n_wide > 0)
        def _():
            across(u).wait_send()

        for t in range(tgt_levels):
            exchange(t, u).wait_send()
        return carry

    lax.fori_loop(0, units, drain, 0)


def solution(mesh):
    n_grp, n_wide = mesh.shape["grp"], mesh.shape["wide"]

    def on_device(coefficients, source_blocks, target_blocks, pair_tables):
        boxes, _, rank, width = coefficients.shape
        tgt_levels = target_blocks.shape[0]
        cols = min(128, width)
        chunks = width // cols
        units = chunks * n_wide
        levels = source_blocks.shape[0] + tgt_levels
        in_vmem = pl.BlockSpec(memory_space=pltpu.VMEM)
        return pl.pallas_call(
            functools.partial(kernel, n_grp, n_wide),
            out_shape=jax.ShapeDtypeStruct(coefficients.shape, jnp.bfloat16),
            in_specs=[pl.BlockSpec(memory_space=pltpu.SMEM)] + [in_vmem] * 3,
            out_specs=in_vmem,
            scratch_shapes=[
                pltpu.VMEM((chunks, boxes, 2, rank, cols), jnp.bfloat16),
                pltpu.VMEM((chunks, boxes, 2, rank, cols), jnp.bfloat16),
                pltpu.VMEM((tgt_levels, units, 2, boxes // n_wide, 2, rank, cols), jnp.bfloat16),
                pltpu.SemaphoreType.DMA((units,)),
                pltpu.SemaphoreType.DMA((units,)),
                pltpu.SemaphoreType.DMA((tgt_levels, units)),
                pltpu.SemaphoreType.DMA((tgt_levels, units)),
            ],
            compiler_params=pltpu.CompilerParams(
                collective_id=0, has_side_effects=True, vmem_limit_bytes=58 * 2**20
            ),
            cost_estimate=pl.CostEstimate(
                flops=levels * boxes * 16 * rank * rank * width,
                bytes_accessed=2 * (2 * coefficients.size + source_blocks.size + target_blocks.size),
                transcendentals=0,
            ),
        )(pair_tables, coefficients, source_blocks, target_blocks)

    in_specs = (
        P(("grp", "wide"), None, None, None),
        P(None, ("grp", "wide"), None, None, None),
        P(None, ("grp", "wide"), None, None, None),
        P(None, ("grp", "wide"), None),
    )
    out_specs = P(("grp", "wide"), None, None, None)
    return jax.shard_map(
        on_device, mesh=mesh, in_specs=in_specs, out_specs=out_specs, check_vma=False
    )
```

time: 314 us -> 147 us (0.47)
  Pallas kernels: 0 us -> 142 us
  waiting for transfers between devices: 97 us -> 0 us
  blocking collectives: 96.9 us -> 0 us
  local copies, waits for them, and re-layouts: 59.6 us -> 4.64 us
  matrix products: 30.7 us -> 0 us
  other arithmetic: 22.6 us -> 0 us
  starting transfers between devices: 4.28 us -> 0 us
    pallas_call x0 -> x1, Pallas kernels: none -> 142 us  [on_device(): pl.pallas_call(functools.partial(kernel, n_grp, n_wide), out_shape=jax.Sh...]
    ppermute x3 -> x0, waiting for transfers between devices: 97 us -> none  [swapped(): return lax.ppermute(value, axis, pairs)]
    all_to_all x1 -> x0, blocking collectives: 96.9 us -> none  [on_device(): lax.all_to_all(current, 'wide', split_axis=0, concat_axis=0, tiled=True)]
    dot_general x20 -> x0, matrix products: 30.7 us -> none  [the longest x5 11.9 us: complex_terms(): jnp.einsum('nij,njk->nik', blocks[:, 1], stacked[:, 0], preferred_element...]
    broadcast_in_dim x2 -> x0, local copies, waits for them, and re-layouts: 12.7 us -> none  [source_level(): joined = jnp.repeat(joined, 2, axis=0)]
    select_n x5 -> x0, other arithmetic: 10.9 us -> none  [the longest x3 5.61 us: target_levels(): upper_part = jnp.where(is_upper, state, partner)]
    gather x2 -> x0, local copies, waits for them, and re-layouts: 10.2 us -> none  [source_level(): picked = jnp.take(local_boxes, order_row, axis=0)]
    concatenate x2 -> x0, local copies, waits for them, and re-layouts: 8.62 us -> none  [source_level(): joined = jnp.concatenate([paired[:, 0], paired[:, 1]], axis=2)]
  transfers between devices with their start and end apart: 3 -> 0, of which waited for: 3 -> 0; matrix products, arithmetic and copies ran while one was open for 3% -> 0% of each run, Pallas kernels for 0% -> 0%
where the time goes in v1:
time: 147 us; the launch traced here: 146 us
  Pallas kernels  142 us (97%)
  local copies, waits for them, and re-layouts  4.64 us (3%)
    pallas_call x1, Pallas kernels, on_device(): pl.pallas_call(functools.partial(kernel, n_grp, n_wide), out_shape=jax.Sh...  142 us
    unnamed x1, local copies, waits for them, and re-layouts  4.64 us

profile of v1, /device:TPU:9, one launch (start us, length us, event | category | flops | bytes accessed | tf_op | source)
XLA Modules:
  0.0 146.5 jit_solution(18030635962614813887)
XLA Ops:
  0.0 141.8 %shard_map.46 = bf16[16,2,128,512]{3,2,1,0:T(8,128)(2,1)} custom-call(s32[2,1,16]{2,1,0:T(1,128)} %tables.1, bf16[16,2,128,512]{3,2,1,0:T(8,128)(2,1)} %coef.1, bf16[2,16,2,128,256]{4,3,2,1,0:T(8,128)(2,1)} %sb.1, bf16[3,16,2,128,256]{4,3,2,1,0:T(8,128)(2,1)} %tb.1), custom_call_target="tpu_custom_call" | custom-call | flops 10737418240 | bytes 18874368 | tf_op jit(solution)/shard_map/pallas_call | solution.py:201
  141.9 4.6 %copy.6 = bf16[16,2,128,512]{3,2,1,0:T(8,128)(2,1)} copy(bf16[16,2,128,512]{3,2,1,0:T(8,128)(2,1)} %shard_map.46) | data formatting | bytes 8388608

commit v2 on v1

--- a/solution.py
+++ b/solution.py
@@ -8,7 +8,7 @@
 from jax.sharding import PartitionSpec as P
 
 MESH = pl.DeviceIdType.MESH
-LOOK_CHUNKS = 2
+LOOK_CHUNKS = 1
 
 
 def flipped(index, other, size):

time: 147 us -> 135 us (0.918)
  Pallas kernels: 142 us -> 131 us
    pallas_call x1, Pallas kernels: 142 us -> 131 us  [on_device(): pl.pallas_call(functools.partial(kernel, n_grp, n_wide), out_shape=jax.Sh...]
where the time goes in v2:
time: 135 us
  Pallas kernels  131 us (97%)
  local copies, waits for them, and re-layouts  4.64 us (3%)
    pallas_call x1, Pallas kernels, on_device(): pl.pallas_call(functools.partial(kernel, n_grp, n_wide), out_shape=jax.Sh...  131 us
    unnamed x1, local copies, waits for them, and re-layouts  4.64 us

profile of v2, /device:TPU:9, one launch (start us, length us, event | category | flops | bytes accessed | tf_op | source)
XLA Modules:
  0.0 135.3 jit_solution(11198568595126551194)
XLA Ops:
  0.0 130.6 %shard_map.46 = bf16[16,2,128,512]{3,2,1,0:T(8,128)(2,1)} custom-call(s32[2,1,16]{2,1,0:T(1,128)} %tables.1, bf16[16,2,128,512]{3,2,1,0:T(8,128)(2,1)} %coef.1, bf16[2,16,2,128,256]{4,3,2,1,0:T(8,128)(2,1)} %sb.1, bf16[3,16,2,128,256]{4,3,2,1,0:T(8,128)(2,1)} %tb.1), custom_call_target="tpu_custom_call" | custom-call | flops 10737418240 | bytes 18874368 | tf_op jit(solution)/shard_map/pallas_call | solution.py:201
  130.6 4.6 %copy.6 = bf16[16,2,128,512]{3,2,1,0:T(8,128)(2,1)} copy(bf16[16,2,128,512]{3,2,1,0:T(8,128)(2,1)} %shard_map.46) | data formatting | bytes 8388608

commit v3 on v2

--- a/solution.py
+++ b/solution.py
@@ -8,7 +8,9 @@
 from jax.sharding import PartitionSpec as P
 
 MESH = pl.DeviceIdType.MESH
-LOOK_CHUNKS = 1
+LOOK = 6
+HOLD = 4
+NEAR = 2
 
 
 def flipped(index, other, size):
@@ -37,8 +39,8 @@
 
 
 def kernel(
-    n_grp, n_wide, tables, coef, sb, tb, out,
-    x1, x2, v, a_send, a_recv, l_send, l_recv,
+    n_grp, n_wide, tables, coef, sb, tb_hbm, out_hbm,
+    tb, tb_sem, out, out_sem, x1, x2, v, a_send, a_recv, l_send, l_recv,
 ):
     boxes, _, rank, width = coef.shape
     src_levels, tgt_levels = sb.shape[0], tb.shape[0]
@@ -51,6 +53,9 @@
     mask = [2 ** (t % bits) for t in range(tgt_levels)]
     side = [(g // b) % 2 for b in mask]
     partner = [g + b * (1 - 2 * s) for b, s in zip(mask, side)]
+
+    blocks_in = pltpu.make_async_copy(tb_hbm, tb, tb_sem)
+    blocks_in.start()
 
     barrier = pltpu.get_barrier_semaphore()
     for d in range(1, n_wide):
@@ -95,6 +100,14 @@
             device_id_type=MESH,
         )
 
+    def result(u):
+        c, d = u // n_wide, u % n_wide
+        base = flipped(w, d, n_wide) * per
+        at = pl.ds(pl.multiple_of(c * cols, cols), cols)
+        return pltpu.make_async_copy(
+            out.at[u], out_hbm.at[pl.ds(base, per), :, :, at], out_sem.at[u]
+        )
+
     def exchange(t, u):
         return pltpu.make_async_remote_copy(
             src_ref=v.at[t, u, side[t]],
@@ -105,38 +118,50 @@
             device_id_type=MESH,
         )
 
-    def send_chunk(c):
-        def step(d, carry):
+    far = n_wide - NEAR
+    n_near, n_far = chunks * NEAR, chunks * far
+    look = min(LOOK, far)
+
+    def far_unit(f):
+        return f // far * n_wide + NEAR + f % far
+
+    def unit(s):
+        late = (s - n_near + units) // units
+        near_u = s // NEAR * n_wide + s % NEAR
+        return (1 - late) * near_u + late * far_unit(s - late * n_near)
+
+    def send_near(c):
+        for d in range(1, NEAR):
             across(c * n_wide + d).start()
-            return carry
-
-        lax.fori_loop(1, n_wide, step, 0)
-
-    look = min(LOOK_CHUNKS, chunks)
-
-    def lead(c, carry):
-        source(c)
-
-        @pl.when(c < look)
-        def _():
-            send_chunk(c)
-
+
+    def arrive(s):
+        u = unit(s)
+
+        @pl.when((s % NEAR == 0) & (s // NEAR + 1 < chunks))
+        def _():
+            source(s // NEAR + 1)
+            send_near(s // NEAR + 1)
+
+        @pl.when(u % n_wide > 0)
+        def _():
+            across(u).wait_recv()
+
+        later = s - HOLD + look
+
+        @pl.when((s >= HOLD) & (later < n_far))
+        def _():
+            across(far_unit(later)).start()
+
+        exchange(0, u).start()
+
+    def first(f, carry):
+        across(far_unit(f)).start()
         return carry
 
-    lax.fori_loop(0, chunks, lead, 0)
-
-    def arrive(u):
-        @pl.when(u % n_wide > 0)
-        def _():
-            across(u).wait_recv()
-
-        later = u + look * n_wide
-
-        @pl.when((u % n_wide > 0) & (later < units))
-        def _():
-            across(later).start()
-
-        exchange(0, u).start()
+    source(0)
+    lax.fori_loop(0, look, first, 0)
+    send_near(0)
+    blocks_in.wait()
 
     def target(t, u):
         exchange(t, u).wait_recv()
@@ -150,11 +175,12 @@
                 v[t + 1, u, side[t + 1], m, 0] = real
                 v[t + 1, u, side[t + 1], m, 1] = imag
             else:
-                at = pl.ds(pl.multiple_of(c * cols, cols), cols)
-                out[base + m, 0, :, at] = real
-                out[base + m, 1, :, at] = imag
+                out[u, m, 0] = real
+                out[u, m, 1] = imag
         if t + 1 < tgt_levels:
             exchange(t + 1, u).start()
+        else:
+            result(u).start()
 
     lags, lag = [], 0
     for t in range(tgt_levels):
@@ -169,7 +195,7 @@
         for t in range(tgt_levels):
             @pl.when((s >= lags[t]) & (s < units + lags[t]))
             def _(t=t):
-                target(t, s - lags[t])
+                target(t, unit(s - lags[t]))
 
         return carry
 
@@ -182,6 +208,7 @@
 
         for t in range(tgt_levels):
             exchange(t, u).wait_send()
+        result(u).wait()
         return carry
 
     lax.fori_loop(0, units, drain, 0)
@@ -201,9 +228,13 @@
         return pl.pallas_call(
             functools.partial(kernel, n_grp, n_wide),
             out_shape=jax.ShapeDtypeStruct(coefficients.shape, jnp.bfloat16),
-            in_specs=[pl.BlockSpec(memory_space=pltpu.SMEM)] + [in_vmem] * 3,
-            out_specs=in_vmem,
+            in_specs=[pl.BlockSpec(memory_space=pltpu.SMEM)] + [in_vmem] * 2 + [pl.BlockSpec(memory_space=pl.ANY)],
+            out_specs=pl.BlockSpec(memory_space=pl.ANY),
             scratch_shapes=[
+                pltpu.VMEM(target_blocks.shape, jnp.bfloat16),
+                pltpu.SemaphoreType.DMA,
+                pltpu.VMEM((units, boxes // n_wide, 2, rank, cols), jnp.bfloat16),
+                pltpu.SemaphoreType.DMA((units,)),
                 pltpu.VMEM((chunks, boxes, 2, rank, cols), jnp.bfloat16),
                 pltpu.VMEM((chunks, boxes, 2, rank, cols), jnp.bfloat16),
                 pltpu.VMEM((tgt_levels, units, 2, boxes // n_wide, 2, rank, cols), jnp.bfloat16),

time: 135 us -> 132 us (0.978)
  Pallas kernels: 131 us -> 127 us
    pallas_call x1, Pallas kernels: 131 us -> 127 us  [on_device(): pl.pallas_call(functools.partial(kernel, n_grp, n_wide), out_shape=jax.Sh...]
where the time goes in v3:
time: 132 us
  Pallas kernels  127 us (96%)
  local copies, waits for them, and re-layouts  4.64 us (4%)
    pallas_call x1, Pallas kernels, on_device(): pl.pallas_call(functools.partial(kernel, n_grp, n_wide), out_shape=jax.Sh...  127 us
    unnamed x1, local copies, waits for them, and re-layouts  4.64 us

profile of v3, /device:TPU:9, one launch (start us, length us, event | category | flops | bytes accessed | tf_op | source)
XLA Modules:
  0.0 132.1 jit_solution(16868142608548212483)
XLA Ops:
  0.0 127.4 %shard_map.46 = bf16[16,2,128,512]{3,2,1,0:T(8,128)(2,1)} custom-call(s32[2,1,16]{2,1,0:T(1,128)} %tables.1, bf16[16,2,128,512]{3,2,1,0:T(8,128)(2,1)} %coef.1, bf16[2,16,2,128,256]{4,3,2,1,0:T(8,128)(2,1)} %sb.1, bf16[3,16,2,128,256]{4,3,2,1,0:T(8,128)(2,1)} %tb_hbm.1), custom_call_target="tpu_custom_call" | custom-call | flops 10737418240 | bytes 18874368 | tf_op jit(solution)/shard_map/pallas_call | solution.py:228
  127.4 4.6 %copy.6 = bf16[16,2,128,512]{3,2,1,0:T(8,128)(2,1)} copy(bf16[16,2,128,512]{3,2,1,0:T(8,128)(2,1)} %shard_map.46) | data formatting | bytes 8388608
